TPU v7x, 32 devices: a whole 2x2x4 slice. The times are simulated.
32 devices in a mesh: groups: 2 (over x), latent: 16 (over z, y, core).
Axes of the slice: x: 2, y: 2, z: 4, core: 2. Of those that a mesh axis runs over, the one named last changes fastest.
Arguments:
- acts: bfloat16 [4096, 8192], P(('groups', 'latent')), parts along dimension 0, may hold values from -6 to 6
- block_ids: int32 [4096, 2], P(('groups', 'latent')), parts along dimension 0, may hold values from 0 to 15, all different within a row; in each aligned block of 128 rows (0 to 127, 128 to 255, ...) at most 32 rows name the same one
- slot_of: int32 [16], replicated, may hold values from 0 to 15, each once
- enc_tiles: bfloat16 [16, 128, 8192], P('latent'), may hold values from -0.0625 to 0.0625
- dec_tiles: bfloat16 [16, 128, 8192], P('latent'), may hold values from -0.375 to 0.375
- enc_bias: float32 [16, 128], P('latent'), may hold values from -3 to 3
- dec_bias: bfloat16 [8192], replicated, may hold values from -3 to 3
Outputs:
- recon: bfloat16 [4096, 8192], P(('groups', 'latent')), parts along dimension 0
- grad_enc: bfloat16 [32, 128, 8192], P(('groups', 'latent')), parts along dimension 0
- grad_dec: bfloat16 [32, 128, 8192], P(('groups', 'latent')), parts along dimension 0
- grad_bias: float32 [32, 128], P(('groups', 'latent')), parts along dimension 0
There are 2 independent parts, one for each index of `groups`. A program takes and returns all parts, laid end to end along the dimension named above; an argument that names none is the same for every part. Nothing has to cross between parts.
Inputs may be any that keep to these rules, and one draw needn't show every extreme that they name: `block_ids`: each row names 2 different blocks. In each aligned block of 128 rows (the rows of one device), no latent block is named by more than 32 rows, and some latent block is named by exactly 32 rows. `slot_of`: A permutation: each slot holds one block.
All inputs are finite; a program needn't handle non-finite values.
Results may differ from a plain program's by a relative error of at most 0.0054.
Values may be sent and summed in bfloat16 or wider, within the bound.
A program may use at most 128 MiB of HBM per device.

v0:
```python
import jax
import jax.numpy as jnp
from jax import lax
from jax.sharding import PartitionSpec as P


def silu_slope(value):
    sig = jax.nn.sigmoid(value)
    return sig * (1.0 + value * (1.0 - sig))


def encode_rows(rows, tile_enc, tile_dec, bias_row, dec_bias):
    pre = jnp.dot(rows, tile_enc.T, preferred_element_type=jnp.float32)
    pre = (
        pre
        - jnp.dot(dec_bias, tile_enc.T, preferred_element_type=jnp.float32)[None, :]
        + bias_row[None, :]
    )
    act = jax.nn.silu(pre).astype(jnp.bfloat16)
    part = jnp.dot(act, tile_dec, preferred_element_type=jnp.float32).astype(jnp.bfloat16)
    return (pre, act, part)


def body(acts, block_ids, slot_of, enc_tiles, dec_tiles, enc_bias, dec_bias):
    devices = lax.axis_size("latent")
    tok_rows, topb = block_ids.shape
    width = acts.shape[1]
    nblk = slot_of.shape[0]
    capacity = 2 * tok_rows * topb // devices
    flat = block_ids.reshape(-1)
    pairs = flat.shape[0]
    picked = flat[:, None] == jnp.arange(nblk, dtype=jnp.int32)[None, :]
    target = jnp.sum(jnp.where(picked, slot_of[None, :], 0), axis=1)
    marks = (target[:, None] == jnp.arange(devices, dtype=jnp.int32)[None, :]).astype(jnp.int32)
    rank = jnp.sum((jnp.cumsum(marks, axis=0) - 1) * marks, axis=1)
    position = target * capacity + rank
    source = jnp.arange(pairs, dtype=jnp.int32) // topb
    outgoing = jnp.zeros((devices * capacity, width), jnp.bfloat16).at[position].set(acts[source])
    outgoing = outgoing.reshape(devices, capacity, width)
    tile_enc = enc_tiles[0]
    tile_dec = dec_tiles[0]
    bias_row = enc_bias[0]
    arrived = lax.all_to_all(outgoing, "latent", split_axis=0, concat_axis=0, tiled=True).reshape(
        devices * capacity, width
    )
    pre, act, part = encode_rows(arrived, tile_enc, tile_dec, bias_row, dec_bias)
    returned = lax.all_to_all(
        part.reshape(devices, capacity, width), "latent", split_axis=0, concat_axis=0, tiled=True
    )
    returned = returned.reshape(devices * capacity, width)
    gathered = returned[position].astype(jnp.float32).reshape(tok_rows, topb, width)
    recon_f = jnp.sum(gathered, axis=1) + dec_bias.astype(jnp.float32)[None, :]
    recon = recon_f.astype(jnp.bfloat16)
    err = (recon_f - acts.astype(jnp.float32)).astype(jnp.bfloat16)
    err_out = jnp.zeros((devices * capacity, width), jnp.bfloat16).at[position].set(err[source])
    errors = lax.all_to_all(
        err_out.reshape(devices, capacity, width), "latent", split_axis=0, concat_axis=0, tiled=True
    )
    errors = errors.reshape(devices * capacity, width)
    slope = jnp.dot(errors, tile_dec.T, preferred_element_type=jnp.float32) * silu_slope(pre)
    slope_b = slope.astype(jnp.bfloat16)
    bias_grad = jnp.sum(slope, axis=0)
    dec_grad = jnp.dot(act.T, errors, preferred_element_type=jnp.float32).astype(jnp.bfloat16)
    enc_grad = jnp.dot(slope_b.T, arrived, preferred_element_type=jnp.float32)
    enc_grad = (enc_grad - bias_grad[:, None] * dec_bias.astype(jnp.float32)[None, :]).astype(
        jnp.bfloat16
    )
    return (recon, enc_grad[None], dec_grad[None], bias_grad[None])


def solution(mesh):
    in_specs = (
        P(("groups", "latent"), None),
        P(("groups", "latent"), None),
        P(),
        P("latent", None, None),
        P("latent", None, None),
        P("latent", None),
        P(),
    )
    out_specs = (
        P(("groups", "latent"), None),
        P(("groups", "latent"), None, None),
        P(("groups", "latent"), None, None),
        P(("groups", "latent"), None),
    )
    return jax.shard_map(body, mesh=mesh, in_specs=in_specs, out_specs=out_specs, check_vma=False)
```

profile of v0, /device:TPU:14, one launch (start us, length us, event | category | flops | bytes accessed | tf_op | source)
XLA Modules:
  0.0 679.8 jit_solution(5790010572581021279)
XLA Ops:
  0.6 0.0 copy-start
  0.7 0.9 copy.11
  1.6 0.1 eq.38
  1.7 0.7 select_reduce_fusion
  2.5 0.6 reduce-window.6
  3.1 0.2 slice_reduce_fusion
  3.3 0.1 fusion.28
  3.4 10.8 %gather_fusion = bf16[256,8192]{1,0:T(8,128)(2,1)} fusion(bf16[128,8192]{1,0:T(8,128)(2,1)} %param.7, s32[1024]{0:T(1024)S(1)} %pad_clamp_fusion.1), kind=kCustom, calls=%fused_computation | custom fusion | bytes 8389632 | tf_op jit(solution)/shard_map/gather | solution.py:38
  14.2 12.8 %scatter_custom_fusion = bf16[512,8192]{1,0:T(8,128)(2,1)} fusion(s32[256]{0:T(256)S(1)} %bitcast.69, bf16[256,8192]{1,0:T(8,128)(2,1)} %gather_fusion, bf16[]{:T(256)} %constant.29.clone.1), kind=kCustom, calls=%fused_computation.14 | custom fusion | bytes 8389120 | tf_op jit(solution)/shard_map/scatter | solution.py:38
  27.0 0.0 copy-start.1
  27.0 0.0 copy-start.3
  27.0 6.4 all-to-all-start
  33.4 0.0 copy-done.1
  33.4 2.2 fusion.23
  35.7 179.9 %all-to-all-done = bf16[16,32,8192]{2,1,0:T(8,128)(2,1)} async-done(((bf16[16,32,8192]{2,1,0:T(8,128)(2,1)}), bf16[16,32,8192]{2,1,0:T(8,128)(2,1)}, u32[]{:S(2)}, u32[]{:S(2)}) %all-to-all-start) | async-done | bytes 8388640 | tf_op jit(solution)/shard_map/all_to_all | solution.py:43
  215.6 0.0 copy-done.3
  215.6 6.3 fusion.20
  221.9 0.0 copy-done
  221.9 5.6 convolution_convert_fusion
  227.5 5.4 all-to-all-start.1
  232.9 182.0 %all-to-all-done.1 = bf16[16,32,8192]{2,1,0:T(8,128)(2,1)} async-done(((bf16[16,32,8192]{2,1,0:T(8,128)(2,1)}), bf16[16,32,8192]{2,1,0:T(8,128)(2,1)}, u32[]{:S(2)}, u32[]{:S(2)}) %all-to-all-start.1) | async-done | bytes 8388640 | tf_op jit(solution)/shard_map/all_to_all | solution.py:47
  414.9 13.4 %gather_fusion.1 = bf16[256,8192]{1,0:T(8,128)(2,1)} fusion(bf16[512,8192]{1,0:T(8,128)(2,1)} %bitcast.13, s32[1024]{0:T(1024)S(1)} %pad_clamp_fusion), kind=kCustom, calls=%fused_computation.1 | custom fusion | bytes 8389632 | tf_op jit(solution)/shard_map/gather | solution.py:51
  428.3 9.7 %reshape.129 = f32[128,2,8192]{2,1,0:T(2,128)} reshape(bf16[256,8192]{1,0:T(8,128)(2,1)} %gather_fusion.1) | data formatting | bytes 12582912 | tf_op jit(solution)/shard_map/convert_element_type | solution.py:51
  438.0 13.5 %reduce_sum.38 = f32[128,8192]{1,0:T(8,128)} reduce(f32[128,2,8192]{2,1,0:T(2,128)} %reshape.129, f32[]{:T(128)} %constant.37.clone.1), dimensions={1}, to_apply=%region_5.6 | reduce | flops 1048576 | bytes 12582916 | tf_op jit(solution)/shard_map/reduce_sum | solution.py:52
  451.5 5.6 subtract_convert_fusion
  457.2 10.8 %gather_fusion.2 = bf16[256,8192]{1,0:T(8,128)(2,1)} fusion(bf16[128,8192]{1,0:T(8,128)(2,1)} %get-tuple-element.4, s32[1024]{0:T(1024)S(1)} %pad_clamp_fusion.1), kind=kCustom, calls=%fused_computation.2 | custom fusion | bytes 8389632 | tf_op jit(solution)/shard_map/gather | solution.py:55
  467.9 12.5 %scatter_custom_fusion.1 = bf16[512,8192]{1,0:T(8,128)(2,1)} fusion(s32[256]{0:T(256)S(1)} %bitcast.71, bf16[256,8192]{1,0:T(8,128)(2,1)} %gather_fusion.2, bf16[]{:T(256)} %constant.29.clone.1), kind=kCustom, calls=%fused_computation.12 | custom fusion | bytes 8389120 | tf_op jit(solution)/shard_map/scatter | solution.py:55
  480.5 187.3 %all_to_all.15 = bf16[16,32,8192]{2,1,0:T(8,128)(2,1)S(1)} all-to-all(bf16[16,32,8192]{2,1,0:T(8,128)(2,1)} %bitcast.67), channel_id=1, replica_groups=mesh['groups'=2,'latent'=16] {'latent'}, dimensions={0} | all-to-all | bytes 16777216 | tf_op jit(solution)/shard_map/all_to_all | solution.py:56
  667.8 2.3 fusion.30
  670.2 0.0 copy-start.2
  670.2 2.7 fusion.1
  672.8 0.0 copy-done.2
  672.8 6.5 fusion.2
  (10 shorter events, 0.1 us)
Async XLA Ops:
  0.6 221.3 %copy-start = (bf16[1,128,8192]{2,1,0:T(8,128)(2,1)S(1)}, bf16[1,128,8192]{2,1,0:T(8,128)(2,1)}, u32[]{:S(2)}) copy-start(bf16[1,128,8192]{2,1,0:T(8,128)(2,1)} %param.11) | copy-start | bytes 6291460
  27.0 6.4 copy-start.1
  27.0 188.6 %copy-start.3 = (f32[1,128]{1,0:T(1,128)S(1)}, f32[1,128]{1,0:T(1,128)}, u32[]{:S(2)}) copy-start(f32[1,128]{1,0:T(1,128)} %param.12) | copy-start | bytes 1540
  27.0 188.6 %all-to-all-start = ((bf16[16,32,8192]{2,1,0:T(8,128)(2,1)}), bf16[16,32,8192]{2,1,0:T(8,128)(2,1)}, u32[]{:S(2)}, u32[]{:S(2)}) async-start(bf16[16,32,8192]{2,1,0:T(8,128)(2,1)} %bitcast.63), calls=%async_computation | async-start | bytes 16777216 | tf_op jit(solution)/shard_map/all_to_all | solution.py:43
  227.5 187.4 %all-to-all-start.1 = ((bf16[16,32,8192]{2,1,0:T(8,128)(2,1)}), bf16[16,32,8192]{2,1,0:T(8,128)(2,1)}, u32[]{:S(2)}, u32[]{:S(2)}) async-start(bf16[16,32,8192]{2,1,0:T(8,128)(2,1)} %bitcast.64), calls=%async_computation.1 | async-start | bytes 16777216 | tf_op jit(solution)/shard_map/all_to_all | solution.py:47
  670.2 2.7 copy-start.2
where the time goes:
time: 689 us; the launch traced here: 680 us
  waiting for transfers between devices  362 us (53%)
  blocking collectives  187 us (27%)
  local copies, waits for them, and re-layouts  71.3 us (10%)
  matrix products  25.6 us (4%)
  other arithmetic  20.6 us (3%)
  starting transfers between devices  11.7 us (2%)
    all_to_all x1, blocking collectives, body(): lax.all_to_all(err_out.reshape(devices, capacity, width), 'latent', split...  187 us
    all_to_all x1, waiting for transfers between devices, body(): lax.all_to_all(part.reshape(devices, capacity, width), 'latent', split_ax...  182 us
    all_to_all x1, waiting for transfers between devices, body(): lax.all_to_all(outgoing, 'latent', split_axis=0, concat_axis=0, tiled=True)  180 us
    scatter x2, local copies, waits for them, and re-layouts, body(): jnp.zeros((devices * capacity, width), jnp.bfloat16).at[position]  25.4 us
  transfers between devices with their start and end apart: 2, of which 2 were waited for; matrix products, arithmetic and copies ran while one was open for 0% of the time, Pallas kernels for 0%

commit v1 on v0

--- a/solution.py
+++ b/solution.py
@@ -1,7 +1,409 @@
+import functools
+
 import jax
 import jax.numpy as jnp
 from jax import lax
+from jax.experimental import pallas as pl
+from jax.experimental.pallas import tpu as pltpu
 from jax.sharding import PartitionSpec as P
+
+BF = jnp.bfloat16
+F32 = jnp.float32
+NT = (((1,), (1,)), ((), ()))
+MESH = pl.DeviceIdType.MESH
+SX, SE, SF, ST, SR, SGD, SGE, SGB = range(8)
+
+
+def place_of(index, nz):
+    return (index % 2) * (2 * nz) + ((index // 2) % 2) * nz + index // 4
+
+
+def device_of(place, nz):
+    return (place % nz) * 4 + ((place // nz) % 2) * 2 + place // (2 * nz)
+
+
+def step_kernel(
+    n,
+    acts,
+    enc,
+    dec,
+    tgt,
+    db_ref,
+    bias_ref,
+    recon_out,
+    genc_out,
+    gdec_out,
+    gb_out,
+    X,
+    E,
+    F,
+    TR,
+    TC,
+    PP,
+    R1,
+    R2,
+    R3,
+    ACT,
+    ACTT,
+    ERR,
+    RO,
+    GD,
+    GE,
+    PRE,
+    GB,
+    GT,
+    send,
+    recv,
+    ar_send,
+    ar_recv,
+    local,
+):
+    nz = n // 4
+    rows = acts.shape[0]
+    cols = acts.shape[1] // n
+    lat = enc.shape[0]
+    me = lax.axis_index("latent")
+    c = me % 2
+    y = (me // 2) % 2
+    z = me // 4
+    mine = place_of(me, nz)
+
+    def far(off):
+        place = (mine + off) % n
+        return place, device_of(place, nz)
+
+    def remote(src, dst, ssem, rsem, dev):
+        return pltpu.make_async_remote_copy(
+            src_ref=src, dst_ref=dst, send_sem=ssem, recv_sem=rsem,
+            device_id={"latent": dev}, device_id_type=MESH,
+        )
+
+    def colpiece(place):
+        return pl.ds(pl.multiple_of(place * cols, cols), cols)
+
+    def rowpiece(place, size=rows):
+        return pl.ds(pl.multiple_of(place * size, size), size)
+
+    def lanepiece(place):
+        return pl.ds(pl.multiple_of(place * rows, rows), rows)
+
+    def each(fn):
+        def go(off, carry):
+            fn(off)
+            return carry
+
+        lax.fori_loop(1, n, go, 0)
+
+    barrier = pltpu.get_barrier_semaphore()
+
+    def greet(off):
+        pl.semaphore_signal(barrier, inc=1, device_id={"latent": far(off)[1]}, device_id_type=MESH)
+
+    each(greet)
+    pl.semaphore_wait(barrier, n - 1)
+
+    def inbound(kind, src, dst):
+        def make(off):
+            place, dev = far(off)
+            return remote(src.at[:, colpiece(place)], dst.at[rowpiece(mine)],
+                          send.at[kind, off], recv.at[kind, off], dev)
+
+        return make
+
+    def tcopy(off):
+        place, dev = far(off)
+        return remote(tgt, TR.at[:, lanepiece(mine)], send.at[ST, off], recv.at[ST, off], dev)
+
+    xcopy = inbound(SX, acts, X)
+    ecopy = inbound(SE, enc, E)
+    fcopy = inbound(SF, dec, F)
+    each(lambda off: tcopy(off).start())
+    each(lambda off: xcopy(off).start())
+    each(lambda off: ecopy(off).start())
+    own = [
+        pltpu.make_async_copy(acts.at[:, colpiece(mine)], X.at[rowpiece(mine)], local.at[0]),
+        pltpu.make_async_copy(enc.at[:, colpiece(mine)], E.at[rowpiece(mine)], local.at[1]),
+        pltpu.make_async_copy(dec.at[:, colpiece(mine)], F.at[rowpiece(mine)], local.at[2]),
+        pltpu.make_async_copy(tgt, TR.at[:, lanepiece(mine)], local.at[3]),
+    ]
+    for copy in own:
+        copy.start()
+    for copy in own:
+        copy.wait()
+    each(lambda off: tcopy(off).wait())
+    each(lambda off: xcopy(off).wait_send())
+    each(lambda off: ecopy(off).wait_send())
+    each(lambda off: fcopy(off).start())
+
+    def columns(p, carry):
+        TC[rowpiece(p), :] = jnp.transpose(TR[:, lanepiece(p)])
+        return carry
+
+    lax.fori_loop(0, n, columns, 0)
+    each(lambda off: xcopy(off).wait_recv())
+    each(lambda off: ecopy(off).wait_recv())
+
+    db = db_ref[...]
+    db_row = db[0:1, :]
+    corr = bias_ref[...] - lax.dot_general(db.astype(BF), E[...], NT, preferred_element_type=F32)
+    corr_row = corr[0:1, :]
+    block = 2 * rows
+
+    def pick(r, full):
+        for j in range(2):
+            t = TC[r, j : j + 1]
+            total = jnp.zeros((block, lat), F32)
+            for s in range(n):
+                total = jnp.where(t == float(s), full[:, s * lat : (s + 1) * lat], total)
+            PP[r, j * lat : (j + 1) * lat] = total
+
+    def encode(i, carry):
+        r = rowpiece(i, block)
+        full = lax.dot_general(X[r, :], E[...], NT, preferred_element_type=F32) + corr_row
+        pick(r, full)
+        return carry
+
+    lax.fori_loop(0, n // 2, encode, 0)
+
+    def reduce_own(phase, after_first, after_third):
+        peer_c, peer_y = z * 4 + y * 2 + (1 - c), z * 4 + (1 - y) * 2 + c
+        half, quarter = 2 * nz * rows, nz * rows
+        one = remote(PP.at[rowpiece(1 - c, half)], R1.at[phase], ar_send.at[phase, 0], ar_recv.at[phase, 0], peer_c)
+        one.start()
+        after_first()
+        one.wait()
+        mine_half = c * 2
+
+        def add(base_rows, buffer, pieces):
+            def go(i, carry):
+                r = rowpiece(base_rows + i)
+                PP[r, :] = PP[r, :] + buffer[phase, rowpiece(i), :]
+                return carry
+
+            lax.fori_loop(0, pieces, go, 0)
+
+        add(c * 2 * nz, R1, 2 * nz)
+        two = remote(PP.at[rowpiece(mine_half + 1 - y, quarter)], R2.at[phase], ar_send.at[phase, 1], ar_recv.at[phase, 1], peer_y)
+        two.start()
+        two.wait()
+        add((mine_half + y) * nz, R2, nz)
+        third = []
+        for dz in range(1, nz):
+            oz = (z + dz) % nz
+            copy = remote(PP.at[rowpiece((mine_half + y) * nz + oz)], R3.at[phase, dz - 1],
+                          ar_send.at[phase, 1 + dz], ar_recv.at[phase, 1 + dz], oz * 4 + y * 2 + c)
+            copy.start()
+            third.append(copy)
+        after_third()
+        for copy in third:
+            copy.wait()
+        total = PP[rowpiece(mine), :]
+        for dz in range(1, nz):
+            total = total + R3[phase, dz - 1]
+        return total
+
+    def spread(phase, between=lambda: None):
+        peer_c, peer_y = z * 4 + y * 2 + (1 - c), z * 4 + (1 - y) * 2 + c
+        half, quarter = 2 * nz * rows, nz * rows
+        base = 1 + nz
+        piece = ACT.at[phase, rowpiece(mine)]
+        copies = []
+        for dz in range(1, nz):
+            oz = (z + dz) % nz
+            copy = remote(piece, piece, ar_send.at[phase, base + dz], ar_recv.at[phase, base + dz], oz * 4 + y * 2 + c)
+            copy.start()
+            copies.append(copy)
+        between()
+        for copy in copies:
+            copy.wait()
+        piece = ACT.at[phase, rowpiece(c * 2 + y, quarter)]
+        copy = remote(piece, piece, ar_send.at[phase, base + nz], ar_recv.at[phase, base + nz], peer_y)
+        copy.start()
+        copy.wait()
+        piece = ACT.at[phase, rowpiece(c, half)]
+        copy = remote(piece, piece, ar_send.at[phase, base + nz + 1], ar_recv.at[phase, base + nz + 1], peer_c)
+        copy.start()
+        copy.wait()
+
+    pre = reduce_own(0, lambda: None, lambda: None)
+    PRE[...] = pre
+    ACT[0, rowpiece(mine), :] = (pre / (1.0 + jnp.exp(-pre))).astype(BF)
+    spread(0)
+
+    each(lambda off: fcopy(off).wait())
+
+    def decode(i, carry):
+        r = rowpiece(i, block)
+        act = ACT[0, r, :]
+        t0, t1 = TC[r, 0:1], TC[r, 1:2]
+        a0, a1 = act[:, :lat].astype(F32), act[:, lat:].astype(F32)
+        wide = jnp.concatenate(
+            [jnp.where(t0 == float(s), a0, jnp.where(t1 == float(s), a1, 0.0)).astype(BF) for s in range(n)],
+            axis=1,
+        )
+        recon_f = jnp.dot(wide, F[...], preferred_element_type=F32) + db_row
+        RO[r, :] = recon_f.astype(BF)
+        err = (recon_f - X[r, :].astype(F32)).astype(BF)
+        ERR[r, :] = err
+        pick(r, lax.dot_general(err, F[...], NT, preferred_element_type=F32))
+        return carry
+
+    lax.fori_loop(0, n // 2, decode, 0)
+
+    def outbound(kind, src, dst):
+        def make(off):
+            place, dev = far(off)
+            return remote(src.at[rowpiece(place)], dst.at[:, colpiece(mine)],
+                          send.at[kind, off], recv.at[kind, off], dev)
+
+        return make
+
+    def keep(src, dst, slot):
+        return pltpu.make_async_copy(src.at[rowpiece(mine)], dst.at[:, colpiece(mine)], local.at[slot])
+
+    rcopy = outbound(SR, RO, recon_out)
+    dcopy = outbound(SGD, GD, gdec_out)
+    gcopy = outbound(SGE, GE, genc_out)
+    keeps = [keep(RO, recon_out, 4), keep(GD, gdec_out, 5), keep(GE, genc_out, 6)]
+
+    def turn(phase):
+        def go(p, carry):
+            ACTT[:, lanepiece(p)] = jnp.transpose(ACT[phase, rowpiece(p), :].astype(F32)).astype(BF)
+            return carry
+
+        lax.fori_loop(0, n, go, 0)
+
+    def grad_tile(s, other):
+        sf = s.astype(F32)
+        t0, t1 = TR[0:1, :], TR[1:2, :]
+        picked = jnp.where(
+            t0 == sf,
+            ACTT[:lat, :].astype(F32),
+            jnp.where(t1 == sf, ACTT[lat:, :].astype(F32), 0.0),
+        ).astype(BF)
+        return jnp.dot(picked, other[...], preferred_element_type=F32)
+
+    def decoder_grad():
+        turn(0)
+
+        def go(s, carry):
+            GD[rowpiece(s), :] = grad_tile(s, ERR).astype(BF)
+            return carry
+
+        lax.fori_loop(0, n, go, 0)
+
+    def first():
+        each(lambda off: rcopy(off).start())
+        keeps[0].start()
+        decoder_grad()
+
+    def third():
+        each(lambda off: dcopy(off).start())
+        keeps[1].start()
+
+    slope = reduce_own(1, first, third)
+    value = PRE[...]
+    sig = 1.0 / (1.0 + jnp.exp(-value))
+    dpre = slope * (sig * (1.0 + value * (1.0 - sig)))
+    ACT[1, rowpiece(mine), :] = dpre.astype(BF)
+    t0, t1 = TC[rowpiece(mine), 0:1], TC[rowpiece(mine), 1:2]
+    for s in range(n):
+        share = jnp.where(t0 == float(s), dpre[:, :lat], 0.0) + jnp.where(t1 == float(s), dpre[:, lat:], 0.0)
+        GT[s : s + 1, :] = jnp.sum(share, axis=0, keepdims=True)
+
+    def bcopy(off):
+        place, dev = far(off)
+        return remote(GT, GB.at[mine], send.at[SGB, off], recv.at[SGB, off], dev)
+
+    each(lambda off: bcopy(off).start())
+    spread(1)
+    GB[mine] = GT[...]
+    each(lambda off: bcopy(off).wait())
+    grad_b = jnp.sum(GB[...], axis=0)
+    grad_cols = jnp.transpose(grad_b)
+    gb_out[...] = grad_b
+    turn(1)
+
+    def encoder_grad(s, carry):
+        lane = lax.broadcasted_iota(jnp.int32, (lat, n), 1)
+        col = jnp.sum(jnp.where(lane == s, grad_cols, 0.0), axis=1, keepdims=True)
+        GE[rowpiece(s), :] = (grad_tile(s, X) - col * db_row).astype(BF)
+        return carry
+
+    lax.fori_loop(0, n, encoder_grad, 0)
+    each(lambda off: gcopy(off).start())
+    keeps[2].start()
+    each(lambda off: rcopy(off).wait())
+    each(lambda off: dcopy(off).wait())
+    each(lambda off: gcopy(off).wait())
+    for copy in keeps:
+        copy.wait()
+
+
+def sliced_body(acts, block_ids, slot_of, enc_tiles, dec_tiles, enc_bias, dec_bias):
+    n = lax.axis_size("latent")
+    nz = n // 4
+    rows, width = acts.shape
+    lat = enc_tiles.shape[1]
+    cols = width // n
+    me = lax.axis_index("latent")
+    mine = place_of(me, nz)
+    picked = block_ids[:, :, None] == jnp.arange(n, dtype=jnp.int32)[None, None, :]
+    target = jnp.sum(jnp.where(picked, place_of(slot_of, nz)[None, None, :], 0), axis=2)
+    tgt = jnp.zeros((8, rows), F32).at[:2].set(target.T.astype(F32))
+    db = lax.dynamic_slice(dec_bias, (mine * cols,), (cols,)).astype(F32)
+    db = jnp.broadcast_to(db[None, :], (8, cols))
+    here = jnp.arange(n, dtype=jnp.int32) == mine
+    bias = jnp.where(here[:, None], enc_bias[0][None, :], 0.0).reshape(1, n * lat)
+    bias = jnp.broadcast_to(bias, (8, n * lat))
+    hbm = pl.BlockSpec(memory_space=pl.ANY)
+    vmem = pl.BlockSpec(memory_space=pltpu.VMEM)
+    all_rows = n * rows
+    sem = pltpu.SemaphoreType.DMA
+    recon, genc, gdec, gb = pl.pallas_call(
+        functools.partial(step_kernel, n),
+        out_shape=(
+            jax.ShapeDtypeStruct((rows, width), BF),
+            jax.ShapeDtypeStruct((lat, width), BF),
+            jax.ShapeDtypeStruct((lat, width), BF),
+            jax.ShapeDtypeStruct((n, lat), F32),
+        ),
+        in_specs=[hbm, hbm, hbm, vmem, vmem, vmem],
+        out_specs=(hbm, hbm, hbm, vmem),
+        scratch_shapes=[
+            pltpu.VMEM((all_rows, cols), BF),
+            pltpu.VMEM((n * lat, cols), BF),
+            pltpu.VMEM((n * lat, cols), BF),
+            pltpu.VMEM((8, all_rows), F32),
+            pltpu.VMEM((all_rows, 8), F32),
+            pltpu.VMEM((all_rows, 2 * lat), F32),
+            pltpu.VMEM((2, all_rows // 2, 2 * lat), F32),
+            pltpu.VMEM((2, all_rows // 4, 2 * lat), F32),
+            pltpu.VMEM((2, nz - 1, rows, 2 * lat), F32),
+            pltpu.VMEM((2, all_rows, 2 * lat), BF),
+            pltpu.VMEM((2 * lat, all_rows), BF),
+            pltpu.VMEM((all_rows, cols), BF),
+            pltpu.VMEM((all_rows, cols), BF),
+            pltpu.VMEM((n * lat, cols), BF),
+            pltpu.VMEM((n * lat, cols), BF),
+            pltpu.VMEM((rows, 2 * lat), F32),
+            pltpu.VMEM((n, n, lat), F32),
+            pltpu.VMEM((n, lat), F32),
+            sem((8, n)),
+            sem((8, n)),
+            sem((2, 4 + 2 * nz)),
+            sem((2, 4 + 2 * nz)),
+            sem((8,)),
+        ],
+        compiler_params=pltpu.CompilerParams(
+            collective_id=0, has_side_effects=True, vmem_limit_bytes=56 * 1024 * 1024
+        ),
+        cost_estimate=pl.CostEstimate(
+            flops=5 * 2 * all_rows * n * lat * cols, bytes_accessed=24 << 20, transcendentals=0
+        ),
+    )(acts, enc_tiles[0], dec_tiles[0], tgt, db, bias)
+    bias_grad = jnp.sum(jnp.where(here[:, None], gb, 0.0), axis=0)
+    return (recon, genc[None], gdec[None], bias_grad[None])
 
 
 def silu_slope(value):
@@ -21,7 +423,7 @@
     return (pre, act, part)
 
 
-def body(acts, block_ids, slot_of, enc_tiles, dec_tiles, enc_bias, dec_bias):
+def routed_body(acts, block_ids, slot_of, enc_tiles, dec_tiles, enc_bias, dec_bias):
     devices = lax.axis_size("latent")
     tok_rows, topb = block_ids.shape
     width = acts.shape[1]
@@ -68,6 +470,13 @@
     return (recon, enc_grad[None], dec_grad[None], bias_grad[None])
 
 
+def body(acts, block_ids, slot_of, enc_tiles, dec_tiles, enc_bias, dec_bias):
+    devices = lax.axis_size("latent")
+    small = devices == 16 and block_ids.shape[1] == 2 and slot_of.shape[0] == devices
+    chosen = sliced_body if small else routed_body
+    return chosen(acts, block_ids, slot_of, enc_tiles, dec_tiles, enc_bias, dec_bias)
+
+
 def solution(mesh):
     in_specs = (
         P(("groups", "latent"), None),

time: 689 us -> 392 us (0.57); the launches traced: 680 us -> 392 us
  Pallas kernels: 0 us -> 378 us
  waiting for transfers between devices: 362 us -> 0 us
  blocking collectives: 187 us -> 0 us
  local copies, waits for them, and re-layouts: 71.3 us -> 8.75 us
  matrix products: 25.6 us -> 0 us
  other arithmetic: 20.6 us -> 4.23 us
  starting transfers between devices: 11.7 us -> 0 us
    pallas_call x0 -> x1, Pallas kernels: none -> 378 us  [sliced_body(): pl.pallas_call(functools.partial(step_kernel, n), out_shape=(jax.ShapeDty...]
    all_to_all x2 -> x0, waiting for transfers between devices: 362 us -> none  [the longest x1 182 us: body(): lax.all_to_all(part.reshape(devices, capacity, width), 'latent', split_ax...]
    all_to_all x1 -> x0, blocking collectives: 187 us -> none  [body(): lax.all_to_all(err_out.reshape(devices, capacity, width), 'latent', split...]
    gather x3 -> x0, local copies, waits for them, and re-layouts: 34.9 us -> none  [the longest x1 13.4 us: body(): returned[position].astype(jnp.float32).reshape(tok_rows, topb, width)]
    dot_general x6 -> x0, matrix products: 25.6 us -> none  [the longest x1 6.46 us: body(): enc_grad = jnp.dot(slope_b.T, arrived, preferred_element_type=jnp.float32)]
    scatter x2 -> x1, local copies, waits for them, and re-layouts: 25.4 us -> 0.6 us  [sliced_body(): tgt = jnp.zeros((8, rows), F32).at[:2].set(target.T.astype(F32))]
    reduce_sum x3 -> x2, other arithmetic: 14.4 us -> 2.06 us  [the longest x1 1.29 us: sliced_body(): bias_grad = jnp.sum(jnp.where(here[:, None], gb, 0.0), axis=0)]
    all_to_all x2 -> x0, starting transfers between devices: 11.7 us -> none  [the longest x1 6.37 us: body(): lax.all_to_all(outgoing, 'latent', split_axis=0, concat_axis=0, tiled=True)]
  transfers between devices with their start and end apart: 2 -> 0, of which waited for: 2 -> 0; matrix products, arithmetic and copies ran while one was open for 0% -> 0% of each run, Pallas kernels for 0% -> 0%
where the time goes in v1:
time: 392 us
  Pallas kernels  378 us (96%)
  local copies, waits for them, and re-layouts  8.75 us (2%)
  other arithmetic  4.23 us (1%)
    pallas_call x1, Pallas kernels, sliced_body(): pl.pallas_call(functools.partial(step_kernel, n), out_shape=(jax.ShapeDty...  378 us

profile of v1, /device:TPU:14, one launch (start us, length us, event | category | flops | bytes accessed | tf_op | source)
XLA Modules:
  0.0 391.5 jit_solution(11366630177367709956)
XLA Ops:
  0.7 0.7 fusion.2
  1.4 0.8 select_reduce_fusion
  2.1 0.8 dynamic-slice_convert_fusion
  2.9 0.6 scatter.4.tgt
  3.5 0.7 select_bitcast_fusion
  4.2 0.6 broadcast_in_dim.70.db_ref
  4.8 0.6 broadcast_in_dim.75.bias_ref
  5.5 377.9 %shard_map.102 = (bf16[128,8192]{1,0:T(8,128)(2,1)}, bf16[128,8192]{1,0:T(8,128)(2,1)}, bf16[128,8192]{1,0:T(8,128)(2,1)}, f32[16,128]{1,0:T(8,128)}) custom-call(bf16[128,8192]{1,0:T(8,128)(2,1)} %acts.1, bf16[128,8192]{1,0:T(8,128)(2,1)} %bitcast.14, bf16[128,8192]{1,0:T(8,128)(2,1)} %bitcast.15, f32[8,128]{1,0:T(8,128)} %scatter.4.tgt, ...), custom_call_target="tpu_custom_call" | custom-call | flops 21474836480 | bytes 25165824 | tf_op jit(solution)/shard_map/pallas_call | solution.py:363
  383.3 1.3 select_reduce_fusion.1
  384.6 0.0 copy-start.1
  384.6 3.2 copy.15
  387.9 0.0 copy-done.1
  387.9 0.0 copy-start
  387.9 1.3 copy.16
  389.2 1.0 copy-done
  390.2 1.3 copy.17
  (2 shorter events, 0.0 us)
Async XLA Ops:
  384.6 3.2 copy-start.1
  387.9 2.3 copy-start

commit v2 on v1

--- a/solution.py
+++ b/solution.py
@@ -11,7 +11,7 @@
 F32 = jnp.float32
 NT = (((1,), (1,)), ((), ()))
 MESH = pl.DeviceIdType.MESH
-SX, SE, SF, ST, SR, SGD, SGE, SGB = range(8)
+SX, SE, SF, ST, SR, SGD, SGE, SGB, SEX, SFX = range(10)
 
 
 def place_of(index, nz):
@@ -67,6 +67,8 @@
     y = (me // 2) % 2
     z = me // 4
     mine = place_of(me, nz)
+    g = lax.axis_index("groups")
+    share = lat // 2
 
     def far(off):
         place = (mine + off) % n
@@ -100,7 +102,9 @@
         pl.semaphore_signal(barrier, inc=1, device_id={"latent": far(off)[1]}, device_id_type=MESH)
 
     each(greet)
-    pl.semaphore_wait(barrier, n - 1)
+    twin = {"groups": 1 - g, "latent": me}
+    pl.semaphore_signal(barrier, inc=1, device_id=twin, device_id_type=MESH)
+    pl.semaphore_wait(barrier, n)
 
     def inbound(kind, src, dst):
         def make(off):
@@ -110,16 +114,39 @@
 
         return make
 
+    def tile_rows(place):
+        return pl.ds(pl.multiple_of(place * lat + g * share, share), share)
+
+    def tile_inbound(kind, src, dst):
+        def make(off):
+            place, dev = far(off)
+            return remote(src.at[pl.ds(pl.multiple_of(g * share, share), share), colpiece(place)],
+                          dst.at[tile_rows(mine)], send.at[kind, off], recv.at[kind, off], dev)
+
+        return make
+
+    def tile_forward(kind, dst):
+        def make(off):
+            piece = dst.at[tile_rows((mine - off + n) % n)]
+            return pltpu.make_async_remote_copy(
+                src_ref=piece, dst_ref=piece, send_sem=send.at[kind, off], recv_sem=recv.at[kind, off],
+                device_id=twin, device_id_type=MESH,
+            )
+
+        return make
+
     def tcopy(off):
         place, dev = far(off)
         return remote(tgt, TR.at[:, lanepiece(mine)], send.at[ST, off], recv.at[ST, off], dev)
 
     xcopy = inbound(SX, acts, X)
-    ecopy = inbound(SE, enc, E)
-    fcopy = inbound(SF, dec, F)
+    ecopy = tile_inbound(SE, enc, E)
+    fcopy = tile_inbound(SF, dec, F)
+    ecross = tile_forward(SEX, E)
+    fcross = tile_forward(SFX, F)
     each(lambda off: tcopy(off).start())
+    each(lambda off: ecopy(off).start())
     each(lambda off: xcopy(off).start())
-    each(lambda off: ecopy(off).start())
     own = [
         pltpu.make_async_copy(acts.at[:, colpiece(mine)], X.at[rowpiece(mine)], local.at[0]),
         pltpu.make_async_copy(enc.at[:, colpiece(mine)], E.at[rowpiece(mine)], local.at[1]),
@@ -131,17 +158,21 @@
     for copy in own:
         copy.wait()
     each(lambda off: tcopy(off).wait())
-    each(lambda off: xcopy(off).wait_send())
-    each(lambda off: ecopy(off).wait_send())
-    each(lambda off: fcopy(off).start())
+
+    def pass_on(copy, cross):
+        def go(off):
+            copy(off).wait_recv()
+            cross(off).start()
+
+        return go
 
     def columns(p, carry):
         TC[rowpiece(p), :] = jnp.transpose(TR[:, lanepiece(p)])
         return carry
 
     lax.fori_loop(0, n, columns, 0)
-    each(lambda off: xcopy(off).wait_recv())
-    each(lambda off: ecopy(off).wait_recv())
+    each(pass_on(ecopy, ecross))
+    each(lambda off: ecross(off).wait())
 
     db = db_ref[...]
     db_row = db[0:1, :]
@@ -158,7 +189,22 @@
             PP[r, j * lat : (j + 1) * lat] = total
 
     def encode(i, carry):
-        r = rowpiece(i, block)
+        b = (mine // 2 - i + n) % (n // 2)
+
+        @pl.when(i == n // 2 - 2)
+        def _():
+            each(lambda off: ecopy(off).wait_send())
+            each(lambda off: xcopy(off).wait_send())
+            each(lambda off: fcopy(off).start())
+
+        for q in range(2):
+            off = (mine - 2 * b - q + n) % n
+
+            @pl.when(off != 0)
+            def _():
+                xcopy(off).wait_recv()
+
+        r = rowpiece(b, block)
         full = lax.dot_general(X[r, :], E[...], NT, preferred_element_type=F32) + corr_row
         pick(r, full)
         return carry
@@ -225,15 +271,33 @@
         copy.start()
         copy.wait()
 
-    pre = reduce_own(0, lambda: None, lambda: None)
+    pre = reduce_own(0, lambda: None, lambda: each(pass_on(fcopy, fcross)))
     PRE[...] = pre
     ACT[0, rowpiece(mine), :] = (pre / (1.0 + jnp.exp(-pre))).astype(BF)
     spread(0)
 
-    each(lambda off: fcopy(off).wait())
+    each(lambda off: fcopy(off).wait_send())
+    each(lambda off: fcross(off).wait())
+
+    def outbound(kind, src, dst):
+        def make(off):
+            place, dev = far(off)
+            return remote(src.at[rowpiece(place)], dst.at[:, colpiece(mine)],
+                          send.at[kind, off], recv.at[kind, off], dev)
+
+        return make
+
+    def keep(src, dst, slot):
+        return pltpu.make_async_copy(src.at[rowpiece(mine)], dst.at[:, colpiece(mine)], local.at[slot])
+
+    rcopy = outbound(SR, RO, recon_out)
+    dcopy = outbound(SGD, GD, gdec_out)
+    gcopy = outbound(SGE, GE, genc_out)
+    keeps = [keep(RO, recon_out, 4), keep(GD, gdec_out, 5), keep(GE, genc_out, 6)]
 
     def decode(i, carry):
-        r = rowpiece(i, block)
+        b = (mine // 2 + i) % (n // 2)
+        r = rowpiece(b, block)
         act = ACT[0, r, :]
         t0, t1 = TC[r, 0:1], TC[r, 1:2]
         a0, a1 = act[:, :lat].astype(F32), act[:, lat:].astype(F32)
@@ -243,6 +307,13 @@
         )
         recon_f = jnp.dot(wide, F[...], preferred_element_type=F32) + db_row
         RO[r, :] = recon_f.astype(BF)
+        for q in range(2):
+            off = (2 * b + q - mine + n) % n
+
+            @pl.when(off != 0)
+            def _():
+                rcopy(off).start()
+
         err = (recon_f - X[r, :].astype(F32)).astype(BF)
         ERR[r, :] = err
         pick(r, lax.dot_general(err, F[...], NT, preferred_element_type=F32))
@@ -250,22 +321,6 @@
 
     lax.fori_loop(0, n // 2, decode, 0)
 
-    def outbound(kind, src, dst):
-        def make(off):
-            place, dev = far(off)
-            return remote(src.at[rowpiece(place)], dst.at[:, colpiece(mine)],
-                          send.at[kind, off], recv.at[kind, off], dev)
-
-        return make
-
-    def keep(src, dst, slot):
-        return pltpu.make_async_copy(src.at[rowpiece(mine)], dst.at[:, colpiece(mine)], local.at[slot])
-
-    rcopy = outbound(SR, RO, recon_out)
-    dcopy = outbound(SGD, GD, gdec_out)
-    gcopy = outbound(SGE, GE, genc_out)
-    keeps = [keep(RO, recon_out, 4), keep(GD, gdec_out, 5), keep(GE, genc_out, 6)]
-
     def turn(phase):
         def go(p, carry):
             ACTT[:, lanepiece(p)] = jnp.transpose(ACT[phase, rowpiece(p), :].astype(F32)).astype(BF)
@@ -274,7 +329,7 @@
         lax.fori_loop(0, n, go, 0)
 
     def grad_tile(s, other):
-        sf = s.astype(F32)
+        sf = jnp.asarray(s, jnp.int32).astype(F32)
         t0, t1 = TR[0:1, :], TR[1:2, :]
         picked = jnp.where(
             t0 == sf,
@@ -286,14 +341,14 @@
     def decoder_grad():
         turn(0)
 
-        def go(s, carry):
+        def go(off):
+            s = (mine + off) % n
             GD[rowpiece(s), :] = grad_tile(s, ERR).astype(BF)
-            return carry
-
-        lax.fori_loop(0, n, go, 0)
+
+        go(0)
+        each(go)
 
     def first():
-        each(lambda off: rcopy(off).start())
         keeps[0].start()
         decoder_grad()
 
@@ -324,14 +379,18 @@
     gb_out[...] = grad_b
     turn(1)
 
-    def encoder_grad(s, carry):
+    def encoder_grad(off):
+        s = (mine + off) % n
         lane = lax.broadcasted_iota(jnp.int32, (lat, n), 1)
         col = jnp.sum(jnp.where(lane == s, grad_cols, 0.0), axis=1, keepdims=True)
         GE[rowpiece(s), :] = (grad_tile(s, X) - col * db_row).astype(BF)
-        return carry
-
-    lax.fori_loop(0, n, encoder_grad, 0)
-    each(lambda off: gcopy(off).start())
+
+    def encoder_step(off):
+        encoder_grad(off)
+        gcopy(off).start()
+
+    each(encoder_step)
+    encoder_grad(0)
     keeps[2].start()
     each(lambda off: rcopy(off).wait())
     each(lambda off: dcopy(off).wait())
@@ -389,8 +448,8 @@
             pltpu.VMEM((rows, 2 * lat), F32),
             pltpu.VMEM((n, n, lat), F32),
             pltpu.VMEM((n, lat), F32),
-            sem((8, n)),
-            sem((8, n)),
+            sem((10, n)),
+            sem((10, n)),
             sem((2, 4 + 2 * nz)),
             sem((2, 4 + 2 * nz)),
             sem((8,)),
@@ -472,7 +531,7 @@
 
 def body(acts, block_ids, slot_of, enc_tiles, dec_tiles, enc_bias, dec_bias):
     devices = lax.axis_size("latent")
-    small = devices == 16 and block_ids.shape[1] == 2 and slot_of.shape[0] == devices
+    small = lax.axis_size("groups") == 2 and devices == 16 and block_ids.shape[1] == 2 and slot_of.shape[0] == devices
     chosen = sliced_body if small else routed_body
     return chosen(acts, block_ids, slot_of, enc_tiles, dec_tiles, enc_bias, dec_bias)
 

time: 392 us -> 324 us (0.83)
  Pallas kernels: 378 us -> 307 us
    pallas_call x1, Pallas kernels: 378 us -> 307 us  [sliced_body(): pl.pallas_call(functools.partial(step_kernel, n), out_shape=(jax.ShapeDty...]
where the time goes in v2:
time: 324 us; the launch traced here: 321 us
  Pallas kernels  307 us (95%)
  local copies, waits for them, and re-layouts  8.75 us (3%)
  other arithmetic  4.23 us (1%)
    pallas_call x1, Pallas kernels, sliced_body(): pl.pallas_call(functools.partial(step_kernel, n), out_shape=(jax.ShapeDty...  307 us
    unnamed x7, local copies, waits for them, and re-layouts  6.91 us

profile of v2, /device:TPU:14, one launch (start us, length us, event | category | flops | bytes accessed | tf_op | source)
XLA Modules:
  0.0 320.7 jit_solution(3223965519685929118)
XLA Ops:
  0.7 0.7 fusion.2
  1.4 0.8 select_reduce_fusion
  2.1 0.8 dynamic-slice_convert_fusion
  2.9 0.6 scatter.4.tgt
  3.5 0.7 select_bitcast_fusion
  4.2 0.6 broadcast_in_dim.70.db_ref
  4.8 0.6 broadcast_in_dim.75.bias_ref
  5.5 307.1 %shard_map.102 = (bf16[128,8192]{1,0:T(8,128)(2,1)}, bf16[128,8192]{1,0:T(8,128)(2,1)}, bf16[128,8192]{1,0:T(8,128)(2,1)}, f32[16,128]{1,0:T(8,128)}) custom-call(bf16[128,8192]{1,0:T(8,128)(2,1)} %acts.1, bf16[128,8192]{1,0:T(8,128)(2,1)} %bitcast.14, bf16[128,8192]{1,0:T(8,128)(2,1)} %bitcast.15, f32[8,128]{1,0:T(8,128)} %scatter.4.tgt, ...), custom_call_target="tpu_custom_call" | custom-call | flops 21474836480 | bytes 25165824 | tf_op jit(solution)/shard_map/pallas_call | solution.py:422
  312.5 1.3 select_reduce_fusion.1
  313.8 0.0 copy-start.1
  313.8 3.2 %copy.15 = bf16[128,8192]{1,0:T(8,128)(2,1)} copy(bf16[128,8192]{1,0:T(8,128)(2,1)} %get-tuple-element.28) | data formatting | bytes 4194304
  317.1 0.0 copy-done.1
  317.1 0.0 copy-start
  317.1 1.3 copy.16
  318.4 1.0 copy-done
  319.4 1.3 copy.17
  (2 shorter events, 0.0 us)
Async XLA Ops:
  313.8 3.2 %copy-start.1 = (bf16[128,8192]{1,0:T(8,128)(2,1)S(1)}, bf16[128,8192]{1,0:T(8,128)(2,1)}, u32[]{:S(2)}) copy-start(bf16[128,8192]{1,0:T(8,128)(2,1)} %get-tuple-element.21) | copy-start | bytes 6291460
  317.1 2.3 copy-start

commit v3 on v2

--- a/solution.py
+++ b/solution.py
@@ -27,7 +27,8 @@
     acts,
     enc,
     dec,
-    tgt,
+    ids_ref,
+    slot_ref,
     db_ref,
     bias_ref,
     recon_out,
@@ -52,6 +53,7 @@
     PRE,
     GB,
     GT,
+    tgt,
     send,
     recv,
     ar_send,
@@ -144,8 +146,13 @@
     fcopy = tile_inbound(SF, dec, F)
     ecross = tile_forward(SEX, E)
     fcross = tile_forward(SFX, F)
+    each(lambda off: ecopy(off).start())
+    ids = ids_ref[...]
+    named = jnp.zeros(ids.shape, F32)
+    for b in range(n):
+        named = jnp.where(ids == b, place_of(slot_ref[b], nz).astype(F32), named)
+    tgt[...] = named
     each(lambda off: tcopy(off).start())
-    each(lambda off: ecopy(off).start())
     each(lambda off: xcopy(off).start())
     own = [
         pltpu.make_async_copy(acts.at[:, colpiece(mine)], X.at[rowpiece(mine)], local.at[0]),
@@ -174,9 +181,11 @@
     each(pass_on(ecopy, ecross))
     each(lambda off: ecross(off).wait())
 
-    db = db_ref[...]
-    db_row = db[0:1, :]
-    corr = bias_ref[...] - lax.dot_general(db.astype(BF), E[...], NT, preferred_element_type=F32)
+    db_row = db_ref[:, colpiece(mine)].astype(F32)
+    db = jnp.broadcast_to(db_row, (16, cols)).astype(BF)
+    lane_block = lax.broadcasted_iota(jnp.int32, (1, n * lat), 1) // lat
+    bias = jnp.where(lane_block == mine, jnp.concatenate([bias_ref[...]] * n, axis=1), 0.0)
+    corr = bias - lax.dot_general(db, E[...], NT, preferred_element_type=F32)
     corr_row = corr[0:1, :]
     block = 2 * rows
 
@@ -356,7 +365,7 @@
         each(lambda off: dcopy(off).start())
         keeps[1].start()
 
-    slope = reduce_own(1, first, third)
+    slope = reduce_own(1, first, lambda: None)
     value = PRE[...]
     sig = 1.0 / (1.0 + jnp.exp(-value))
     dpre = slope * (sig * (1.0 + value * (1.0 - sig)))
@@ -371,12 +380,13 @@
         return remote(GT, GB.at[mine], send.at[SGB, off], recv.at[SGB, off], dev)
 
     each(lambda off: bcopy(off).start())
-    spread(1)
+    spread(1, third)
     GB[mine] = GT[...]
     each(lambda off: bcopy(off).wait())
     grad_b = jnp.sum(GB[...], axis=0)
     grad_cols = jnp.transpose(grad_b)
-    gb_out[...] = grad_b
+    row = lax.broadcasted_iota(jnp.int32, (n, lat), 0)
+    gb_out[...] = jnp.sum(jnp.where(row == mine, grad_b, 0.0), axis=0, keepdims=True)
     turn(1)
 
     def encoder_grad(off):
@@ -405,16 +415,7 @@
     rows, width = acts.shape
     lat = enc_tiles.shape[1]
     cols = width // n
-    me = lax.axis_index("latent")
-    mine = place_of(me, nz)
-    picked = block_ids[:, :, None] == jnp.arange(n, dtype=jnp.int32)[None, None, :]
-    target = jnp.sum(jnp.where(picked, place_of(slot_of, nz)[None, None, :], 0), axis=2)
-    tgt = jnp.zeros((8, rows), F32).at[:2].set(target.T.astype(F32))
-    db = lax.dynamic_slice(dec_bias, (mine * cols,), (cols,)).astype(F32)
-    db = jnp.broadcast_to(db[None, :], (8, cols))
-    here = jnp.arange(n, dtype=jnp.int32) == mine
-    bias = jnp.where(here[:, None], enc_bias[0][None, :], 0.0).reshape(1, n * lat)
-    bias = jnp.broadcast_to(bias, (8, n * lat))
+    ids = jnp.pad(block_ids.T, ((0, 6), (0, 0)))
     hbm = pl.BlockSpec(memory_space=pl.ANY)
     vmem = pl.BlockSpec(memory_space=pltpu.VMEM)
     all_rows = n * rows
@@ -425,9 +426,9 @@
             jax.ShapeDtypeStruct((rows, width), BF),
             jax.ShapeDtypeStruct((lat, width), BF),
             jax.ShapeDtypeStruct((lat, width), BF),
-            jax.ShapeDtypeStruct((n, lat), F32),
+            jax.ShapeDtypeStruct((1, lat), F32),
         ),
-        in_specs=[hbm, hbm, hbm, vmem, vmem, vmem],
+        in_specs=[hbm, hbm, hbm, vmem, pl.BlockSpec(memory_space=pltpu.SMEM), vmem, vmem],
         out_specs=(hbm, hbm, hbm, vmem),
         scratch_shapes=[
             pltpu.VMEM((all_rows, cols), BF),
@@ -448,6 +449,7 @@
             pltpu.VMEM((rows, 2 * lat), F32),
             pltpu.VMEM((n, n, lat), F32),
             pltpu.VMEM((n, lat), F32),
+            pltpu.VMEM((8, rows), F32),
             sem((10, n)),
             sem((10, n)),
             sem((2, 4 + 2 * nz)),
@@ -460,9 +462,8 @@
         cost_estimate=pl.CostEstimate(
             flops=5 * 2 * all_rows * n * lat * cols, bytes_accessed=24 << 20, transcendentals=0
         ),
-    )(acts, enc_tiles[0], dec_tiles[0], tgt, db, bias)
-    bias_grad = jnp.sum(jnp.where(here[:, None], gb, 0.0), axis=0)
-    return (recon, genc[None], gdec[None], bias_grad[None])
+    )(acts, enc_tiles[0], dec_tiles[0], ids, slot_of, dec_bias.reshape(1, width), enc_bias)
+    return (recon, genc[None], gdec[None], gb)
 
 
 def silu_slope(value):

time: 324 us -> 311 us (0.960)
  Pallas kernels: 307 us -> 294 us
  other arithmetic: 4.23 us -> 0 us
    pallas_call x1, Pallas kernels: 307 us -> 294 us  [sliced_body(): pl.pallas_call(functools.partial(step_kernel, n), out_shape=(jax.ShapeDty...]
    unnamed x7 -> x10, local copies, waits for them, and re-layouts: 6.91 us -> 7.43 us
where the time goes in v3:
time: 311 us; the launch traced here: 305 us
  Pallas kernels  294 us (95%)
  local copies, waits for them, and re-layouts  10.1 us (3%)
    pallas_call x1, Pallas kernels, sliced_body(): pl.pallas_call(functools.partial(step_kernel, n), out_shape=(jax.ShapeDty...  294 us
    unnamed x10, local copies, waits for them, and re-layouts  7.43 us

profile of v3, /device:TPU:14, one launch (start us, length us, event | category | flops | bytes accessed | tf_op | source)
XLA Modules:
  0.0 304.9 jit_solution(16488356185578992245)
XLA Ops:
  0.6 1.3 pad.4.ids_ref
  1.9 1.3 reshape.11.db_ref
  3.3 294.2 %shard_map.102 = (bf16[128,8192]{1,0:T(8,128)(2,1)}, bf16[128,8192]{1,0:T(8,128)(2,1)}, bf16[128,8192]{1,0:T(8,128)(2,1)}, f32[1,128]{1,0:T(1,128)}) custom-call(bf16[128,8192]{1,0:T(8,128)(2,1)} %acts.1, bf16[128,8192]{1,0:T(8,128)(2,1)} %bitcast.8, bf16[128,8192]{1,0:T(8,128)(2,1)} %bitcast.9, s32[8,128]{1,0:T(8,128)} %pad.4.ids_ref, s32[16]{0:T(128)} %slot_ref.1, ...), custom_call_target="tpu_custom_call" | custom-call | flops 21474836480 | bytes 25165824 | tf_op jit(solution)/shard_map/pallas_call | solution.py:423
  297.5 0.0 copy-start.1
  297.5 3.2 %copy.15 = bf16[128,8192]{1,0:T(8,128)(2,1)} copy(bf16[128,8192]{1,0:T(8,128)(2,1)} %get-tuple-element.16) | data formatting | bytes 4194304
  300.7 0.0 copy-done.1
  300.7 0.0 copy-start
  300.7 1.3 copy.16
  302.1 1.0 copy-done
  303.1 0.0 copy-start.2
  303.1 1.3 copy.17
  304.4 0.0 copy-done.2
  304.4 0.5 copy.18
Async XLA Ops:
  297.5 3.3 %copy-start.1 = (bf16[128,8192]{1,0:T(8,128)(2,1)S(1)}, bf16[128,8192]{1,0:T(8,128)(2,1)}, u32[]{:S(2)}) copy-start(bf16[128,8192]{1,0:T(8,128)(2,1)} %get-tuple-element.9) | copy-start | bytes 6291460
  300.7 2.3 copy-start
  303.1 1.3 copy-start.2
